TPU v7x, 512 devices: a whole 4x4x16 slice. The times are simulated.
512 devices in a mesh: chan: 128 (over y, z, x_hi), pair: 4 (over x_lo, core).
Axes of the slice: x: 4 (x_hi: 2, x_lo: 2; x = x_hi * 2 + x_lo), y: 4, z: 16, core: 2. Of those that a mesh axis runs over, the one named last changes fastest.
Arguments:
- voltages: bfloat16 [4, 256, 2, 34560], P('pair', 'chan'), may hold values from -6 to 6
- fir_taps: float32 [8, 256], replicated, may hold values from -2 to 2
Outputs:
- visibilities: float32 [128, 2, 1024, 1024], P('chan', None, 'pair')
All inputs are finite; a program needn't handle non-finite values.
Results may differ from a plain program's by a relative error of at most 0.0036.
Values may be sent and summed in bfloat16 or wider, within the bound.
A program may use at most 64 MiB of HBM per device.

v0:
```python
import math
import jax
import jax.numpy as jnp
from jax import lax
from jax.sharding import PartitionSpec as P


def dft_rows(channels):
    frame = 2 * channels
    row_index = jnp.arange(2 * channels, dtype=jnp.int32)
    col_index = jnp.arange(frame, dtype=jnp.int32)
    freq_index = row_index // 2
    phases = freq_index[:, None] * col_index[None, :] % frame
    angles = phases.astype(jnp.float32) * (2.0 * math.pi / frame)
    chosen = jnp.where((row_index % 2 == 0)[:, None], jnp.cos(angles), -jnp.sin(angles))
    return chosen * (1.0 / math.sqrt(frame))


def channelize(sample_rows, fir_taps, transform, spectra_len):
    tap_count, frame = fir_taps.shape
    channels = frame // 2
    framed = sample_rows.astype(jnp.float32).reshape(
        sample_rows.shape[0], spectra_len + tap_count - 1, frame
    )
    filtered = jnp.zeros((sample_rows.shape[0], spectra_len, frame), jnp.float32)
    for tap in range(tap_count):
        filtered = filtered + fir_taps[tap][None, None, :] * framed[:, tap : tap + spectra_len, :]
    spectra = jnp.einsum("wn,asn->aws", transform, filtered, precision=lax.Precision.HIGHEST)
    return spectra.reshape(sample_rows.shape[0], channels, 2 * spectra_len).astype(jnp.bfloat16)


def correlate(own_rows, columns, spectra_len):
    blocks = columns.shape[2] // (2 * spectra_len)
    shaped = columns.reshape(columns.shape[0], columns.shape[1], blocks, 2, spectra_len)
    rotated = jnp.stack([-shaped[:, :, :, 1, :], shaped[:, :, :, 0, :]], axis=3).reshape(
        columns.shape
    )
    stacked = jnp.concatenate([columns, rotated], axis=0)
    stacked = jnp.transpose(stacked, (1, 0, 2))
    own_first = jnp.transpose(own_rows, (1, 0, 2))
    product = jnp.einsum("cik,cjk->cij", own_first, stacked, preferred_element_type=jnp.float32)
    count = columns.shape[0]
    product = product.reshape(product.shape[0], product.shape[1], 2, count)
    return jnp.transpose(product, (0, 2, 1, 3))


def shards(voltages, fir_taps):
    samples = voltages[0]
    batch_count = samples.shape[1]
    tap_count, frame = fir_taps.shape
    spectra_len = samples.shape[2] // frame - tap_count + 1
    transform = dft_rows(frame // 2)
    pieces = [
        channelize(samples[:, batch], fir_taps, transform, spectra_len)
        for batch in range(batch_count)
    ]
    spectra = jnp.concatenate(pieces, axis=2)[None]
    gathered = lax.all_gather(spectra, "pair", axis=0, tiled=True)
    turned = lax.all_to_all(gathered, "chan", split_axis=2, concat_axis=1, tiled=True)
    everyone = turned.reshape(turned.shape[0] * turned.shape[1], turned.shape[2], turned.shape[3])
    own_rows = lax.dynamic_index_in_dim(turned, lax.axis_index("pair"), 0, keepdims=False)
    summed = correlate(own_rows, everyone, spectra_len)
    return summed * (1.0 / math.sqrt(batch_count * spectra_len))


def solution(mesh):
    in_specs = (P("pair", "chan", None, None), P())
    out_specs = P("chan", None, "pair", None)
    return jax.shard_map(shards, mesh=mesh, in_specs=in_specs, out_specs=out_specs, check_vma=False)
```

profile of v0, /device:TPU:8, one launch (start us, length us, event | category | flops | bytes accessed | tf_op | source)
XLA Modules:
  0.0 145.8 jit_solution(16215200199921057058)
XLA Ops:
  6.5 1.0 fusion.70
  7.5 2.8 %fusion.3 = (f32[2,34560]{1,0:T(2,128)S(1)}, f32[2,34560]{1,0:T(2,128)S(1)}) fusion(bf16[2,2,34560]{2,1,0:T(2,128)(2,1)} %bitcast.42), kind=kLoop, calls=%fused_computation.14 | loop fusion | flops 138240 | bytes 829440 | tf_op jit(solution)/shard_map/convert_element_type | solution.py:22
  10.4 0.2 reshape.76
  10.6 1.7 %fusion = bf16[2,256,128]{1,2,0:T(8,128)(2,1)S(1)} fusion(f32[2,135,256]{2,1,0:T(8,128)S(1)} %reshape.76, f32[256]{0:T(256)S(1)} %bitcast.56, f32[256]{0:T(256)S(1)} %bitcast.58, f32[256]{0:T(256)S(1)} %bitcast.46, f32[256]{0:T(256)S(1)} %bitcast.48, f32[256]{0:T(256)S(1)} %bitcast.50, f32[256]{0:T(256)S(1)} %bitcast.52, f32[256]{0:T(256)S(1)} %bitcast.54, ...), kind=kOutput, calls=%fused_computation.4 | convolution fusion | flops 203489280 | bytes 2237952 | tf_op jit(solution)/shard_map/wn,asn->aws/dot_general | solution.py:28
  12.4 0.1 copy.15
  12.6 0.2 reshape.77
  12.8 1.7 %fusion.1 = bf16[2,256,128]{1,2,0:T(8,128)(2,1)S(1)} fusion(f32[2,135,256]{2,1,0:T(8,128)S(1)} %reshape.77, f32[256]{0:T(256)S(1)} %bitcast.57, f32[256]{0:T(256)S(1)} %bitcast.59, f32[256]{0:T(256)S(1)} %bitcast.47, f32[256]{0:T(256)S(1)} %bitcast.49, f32[256]{0:T(256)S(1)} %bitcast.51, f32[256]{0:T(256)S(1)} %bitcast.53, f32[256]{0:T(256)S(1)} %bitcast.55, ...), kind=kOutput, calls=%fused_computation.5 | convolution fusion | flops 203489280 | bytes 2237952 | tf_op jit(solution)/shard_map/wn,asn->aws/dot_general | solution.py:28
  14.5 0.1 copy.16
  14.7 0.7 pad_maximum_fusion.2
  15.5 0.0 all-gather.3.cloned.1.call-update
  15.5 32.9 %all-gather.3.cloned.1.call-done = bf16[8,128,512]{2,1,0:T(8,128)(2,1)} async-done(((bf16[2,128,512]{2,1,0:T(8,128)(2,1)}), bf16[8,128,512]{2,1,0:T(8,128)(2,1)}) %all-gather.3.cloned.1.call-update) | async-done | bytes 1048592 | tf_op jit(solution)/shard_map/all_gather | solution.py:58
  48.4 3.3 %copy.17 = bf16[4,2,128,512]{3,1,0,2:T(2,128)(2,1)} copy(bf16[4,2,128,512]{3,2,1,0:T(8,128)(2,1)} %bitcast.43) | data formatting | bytes 2097152 | tf_op jit(solution)/shard_map/all_gather | solution.py:58
  51.6 18.7 %all-to-all-start = ((bf16[4,2,128,512]{3,1,0,2:T(2,128)(2,1)}), bf16[4,2,128,512]{3,1,0,2:T(2,128)(2,1)S(1)}, u32[]{:S(2)}, u32[]{:S(2)}) async-start(bf16[4,2,128,512]{3,1,0,2:T(2,128)(2,1)} %copy.17), calls=%async_computation | async-start | bytes 2097152 | tf_op jit(solution)/shard_map/all_to_all | solution.py:59
  70.4 56.0 %all-to-all-done = bf16[4,2,128,512]{3,1,0,2:T(2,128)(2,1)S(1)} async-done(((bf16[4,2,128,512]{3,1,0,2:T(2,128)(2,1)}), bf16[4,2,128,512]{3,1,0,2:T(2,128)(2,1)S(1)}, u32[]{:S(2)}, u32[]{:S(2)}) %all-to-all-start) | async-done | bytes 1048608 | tf_op jit(solution)/shard_map/all_to_all | solution.py:59
  126.4 0.7 copy.19
  127.1 1.4 copy.18
  128.5 0.7 reshape_reshape.3
  129.2 0.4 reshape.74
  129.7 2.3 %slice_negate_fusion = (bf16[1024,1,2,1,128]{4,3,2,0,1:T(2,128)(2,1)S(1)}, bf16[1024,1,2,1,128]{4,3,2,0,1:T(2,128)(2,1)S(1)}) fusion(bf16[1024,1,2,2,128]{4,3,2,0,1:T(2,128)(2,1)S(1)} %reshape_reshape.3), kind=kLoop, calls=%fused_computation.6 | loop fusion | flops 262144 | bytes 2097152 | tf_op jit(solution)/shard_map/neg | solution.py:35
  132.0 2.4 %pad_maximum_fusion.1 = bf16[1024,1,2,2,128]{4,3,2,0,1:T(2,128)(2,1)S(1)} fusion(bf16[1024,1,2,1,128]{4,3,2,0,1:T(2,128)(2,1)S(1)} %get-tuple-element.8, bf16[1024,1,2,1,128]{4,3,2,0,1:T(2,128)(2,1)S(1)} %get-tuple-element.7), kind=kLoop, calls=%fused_computation.7 | loop fusion | flops 2097152 | bytes 2097152 | tf_op jit(solution)/shard_map/stack | solution.py:35
  134.5 0.4 reshape.75
  134.9 1.8 %constant_dynamic-slice_fusion = bf16[1,256,1,512]{3,0,1,2:T(2,128)(2,1)S(1)} fusion(bf16[4,256,1,512]{3,0,1,2:T(4,128)(2,1)} %bitcast.41, s32[]{:T(128)S(6)} %select_n.46), kind=kLoop, calls=%fused_computation.81 | loop fusion | bytes 524292 | tf_op jit(solution)/shard_map/jit(dynamic_index_in_dim)/dynamic_slice | solution.py:61
  136.7 0.1 pad_maximum_fusion
  136.8 2.1 %multiply_bitcast_fusion = f32[1,2,256,1024]{3,2,1,0:T(8,128)} fusion(bf16[2,1024,512]{2,1,0:T(8,128)(2,1)S(1)} %bitcast.40, bf16[1,256,1,512]{3,0,1,2:T(2,128)(2,1)S(1)} %constant_dynamic-slice_fusion), kind=kOutput, calls=%fused_computation.1 | convolution fusion | flops 537395200 | bytes 4456448 | tf_op jit(solution)/shard_map/cik,cjk->cij/dot_general | solution.py:41
  (5 shorter events, 0.1 us)
Async XLA Ops:
  6.5 41.8 %all-gather.3.cloned.1.call-start = ((), (), s32[]{:S(2)}) async-start(), calls=%async_computation.1 | async-start | bytes 1310720 | tf_op jit(solution)/shard_map/all_gather | solution.py:58
  51.6 74.8 %all-to-all-start = ((bf16[4,2,128,512]{3,1,0,2:T(2,128)(2,1)}), bf16[4,2,128,512]{3,1,0,2:T(2,128)(2,1)S(1)}, u32[]{:S(2)}, u32[]{:S(2)}) async-start(bf16[4,2,128,512]{3,1,0,2:T(2,128)(2,1)} %copy.17), calls=%async_computation | async-start | bytes 2097152 | tf_op jit(solution)/shard_map/all_to_all | solution.py:59
Sparse Core Ops, SparseCore 0:
  15.6 32.7 all-gather.2
where the time goes:
time: 146 us
  waiting for transfers between devices  88.9 us (61%)
  starting transfers between devices  18.7 us (13%)
  between operations  13.5 us (9%)
  local copies, waits for them, and re-layouts  10.5 us (7%)
  other arithmetic  8.5 us (6%)
  matrix products  5.56 us (4%)
    all_to_all x1, waiting for transfers between devices, shards(): lax.all_to_all(gathered, 'chan', split_axis=2, concat_axis=1, tiled=True)  56 us
    all_gather x1, waiting for transfers between devices, shards(): gathered = lax.all_gather(spectra, 'pair', axis=0, tiled=True)  32.9 us
    all_to_all x1, starting transfers between devices, shards(): lax.all_to_all(gathered, 'chan', split_axis=2, concat_axis=1, tiled=True)  18.7 us
    dot_general x2, matrix products, channelize(): jnp.einsum('wn,asn->aws', transform, filtered, precision=lax.Precision.HI...  3.49 us
    all_gather x1, local copies, waits for them, and re-layouts, shards(): gathered = lax.all_gather(spectra, 'pair', axis=0, tiled=True)  3.27 us
  transfers between devices with their start and end apart: 2, of which 2 were waited for; matrix products, arithmetic and copies ran while one was open for 0% of the time, Pallas kernels for 0%

commit v1 on v0

--- a/solution.py
+++ b/solution.py
@@ -55,7 +55,9 @@
         for batch in range(batch_count)
     ]
     spectra = jnp.concatenate(pieces, axis=2)[None]
-    gathered = lax.all_gather(spectra, "pair", axis=0, tiled=True)
+    gathered = jnp.concatenate(
+        lax.all_to_all(jnp.stack([spectra] * lax.axis_size("pair")), "pair", 0, 0), axis=0
+    )
     turned = lax.all_to_all(gathered, "chan", split_axis=2, concat_axis=1, tiled=True)
     everyone = turned.reshape(turned.shape[0] * turned.shape[1], turned.shape[2], turned.shape[3])
     own_rows = lax.dynamic_index_in_dim(turned, lax.axis_index("pair"), 0, keepdims=False)

time: 146 us -> 118 us (0.81)
  waiting for transfers between devices: 88.9 us -> 55.2 us
  blocking collectives: 0 us -> 17 us
  between operations: 13.5 us -> 0.15 us
  starting transfers between devices: 18.7 us -> 21.9 us
    all_gather x1 -> x0, waiting for transfers between devices: 32.9 us -> none  [shards(): gathered = lax.all_gather(spectra, 'pair', axis=0, tiled=True)]
    all_to_all x0 -> x1, blocking collectives: none -> 17 us  [shards(): lax.all_to_all(jnp.stack([spectra] * lax.axis_size('pair')), 'pair', 0, 0)]
    all_gather x1 -> x0, local copies, waits for them, and re-layouts: 3.27 us -> none  [shards(): gathered = lax.all_gather(spectra, 'pair', axis=0, tiled=True)]
    all_to_all x1, starting transfers between devices: 18.7 us -> 21.9 us  [shards(): lax.all_to_all(gathered, 'chan', split_axis=2, concat_axis=1, tiled=True)]
    reshape x0 -> x1, local copies, waits for them, and re-layouts: none -> 1.69 us  [shards(): jnp.concatenate(lax.all_to_all(jnp.stack([spectra] * lax.axis_size('pair'...]
  transfers between devices with their start and end apart: 2 -> 1, of which waited for: 2 -> 1; matrix products, arithmetic and copies ran while one was open for 0% -> 0% of each run, Pallas kernels for 0% -> 0%
where the time goes in v1:
time: 118 us; the launch traced here: 117 us
  waiting for transfers between devices  55.2 us (47%)
  starting transfers between devices  21.9 us (19%)
  blocking collectives  17 us (14%)
  local copies, waits for them, and re-layouts  9.74 us (8%)
  other arithmetic  7.79 us (7%)
  matrix products  5.56 us (5%)
    all_to_all x1, waiting for transfers between devices, shards(): lax.all_to_all(gathered, 'chan', split_axis=2, concat_axis=1, tiled=True)  55.2 us
    all_to_all x1, starting transfers between devices, shards(): lax.all_to_all(gathered, 'chan', split_axis=2, concat_axis=1, tiled=True)  21.9 us
    all_to_all x1, blocking collectives, shards(): lax.all_to_all(jnp.stack([spectra] * lax.axis_size('pair')), 'pair', 0, 0)  17 us
    dot_general x2, matrix products, channelize(): jnp.einsum('wn,asn->aws', transform, filtered, precision=lax.Precision.HI...  3.49 us
    convert_element_type x1, other arithmetic, channelize(): sample_rows.astype(jnp.float32)  2.85 us
    another operation x1, other arithmetic, correlate(): jnp.stack([-shaped[:, :, :, 1, :], shaped[:, :, :, 0, :]], axis=3)  2.43 us
  transfers between devices with their start and end apart: 1, of which 1 were waited for; matrix products, arithmetic and copies ran while one was open for 0% of the time, Pallas kernels for 0%

profile of v1, /device:TPU:8, one launch (start us, length us, event | category | flops | bytes accessed | tf_op | source)
XLA Modules:
  0.0 117.5 jit_solution(9442558519951687002)
XLA Ops:
  0.0 1.0 fusion.70
  1.0 2.8 %fusion.3 = (f32[2,34560]{1,0:T(2,128)S(1)}, f32[2,34560]{1,0:T(2,128)S(1)}) fusion(bf16[2,2,34560]{2,1,0:T(2,128)(2,1)} %bitcast.43), kind=kLoop, calls=%fused_computation.14 | loop fusion | flops 138240 | bytes 829440 | tf_op jit(solution)/shard_map/convert_element_type | solution.py:22
  3.9 0.2 reshape.82
  4.1 1.7 %fusion = bf16[2,256,128]{1,2,0:T(8,128)(2,1)S(1)} fusion(f32[2,135,256]{2,1,0:T(8,128)S(1)} %reshape.82, f32[256]{0:T(256)S(1)} %bitcast.56, f32[256]{0:T(256)S(1)} %bitcast.58, f32[256]{0:T(256)S(1)} %bitcast.46, f32[256]{0:T(256)S(1)} %bitcast.48, f32[256]{0:T(256)S(1)} %bitcast.50, f32[256]{0:T(256)S(1)} %bitcast.52, f32[256]{0:T(256)S(1)} %bitcast.54, ...), kind=kOutput, calls=%fused_computation.4 | convolution fusion | flops 203489280 | bytes 2237952 | tf_op jit(solution)/shard_map/wn,asn->aws/dot_general | solution.py:28
  5.8 0.1 copy.17
  6.0 0.2 reshape.83
  6.3 1.7 %fusion.1 = bf16[2,256,128]{1,2,0:T(8,128)(2,1)S(1)} fusion(f32[2,135,256]{2,1,0:T(8,128)S(1)} %reshape.83, f32[256]{0:T(256)S(1)} %bitcast.57, f32[256]{0:T(256)S(1)} %bitcast.59, f32[256]{0:T(256)S(1)} %bitcast.47, f32[256]{0:T(256)S(1)} %bitcast.49, f32[256]{0:T(256)S(1)} %bitcast.51, f32[256]{0:T(256)S(1)} %bitcast.53, f32[256]{0:T(256)S(1)} %bitcast.55, ...), kind=kOutput, calls=%fused_computation.5 | convolution fusion | flops 203489280 | bytes 2237952 | tf_op jit(solution)/shard_map/wn,asn->aws/dot_general | solution.py:28
  8.0 0.1 copy.18
  8.2 0.3 copy.19
  8.5 0.5 stack.7
  9.0 17.0 %all_to_all.23 = bf16[4,1,2,128,512]{4,2,3,1,0:T(2,128)(2,1)S(1)} all-to-all(bf16[4,1,2,128,512]{4,2,3,1,0:T(2,128)(2,1)S(1)} %stack.7), channel_id=1, replica_groups=mesh['chan'=128,'pair'=4] {'pair'}, dimensions={0} | all-to-all | bytes 2097152 | tf_op jit(solution)/shard_map/all_to_all | solution.py:59
  26.1 1.7 %copy.20 = bf16[4,2,128,512]{3,1,0,2:T(2,128)(2,1)} copy(bf16[4,2,128,512]{3,1,2,0:T(2,128)(2,1)S(1)} %bitcast.41) | data formatting | bytes 2097152 | tf_op jit(solution)/shard_map/reshape | solution.py:58
  27.8 21.9 %all-to-all-start.1 = ((bf16[4,2,128,512]{3,1,0,2:T(2,128)(2,1)}), bf16[4,2,128,512]{3,1,0,2:T(2,128)(2,1)S(1)}, u32[]{:S(2)}, u32[]{:S(2)}) async-start(bf16[4,2,128,512]{3,1,0,2:T(2,128)(2,1)} %copy.20), calls=%async_computation.1 | async-start | bytes 2097152 | tf_op jit(solution)/shard_map/all_to_all | solution.py:61
  49.7 55.2 %all-to-all-done.1 = bf16[4,2,128,512]{3,1,0,2:T(2,128)(2,1)S(1)} async-done(((bf16[4,2,128,512]{3,1,0,2:T(2,128)(2,1)}), bf16[4,2,128,512]{3,1,0,2:T(2,128)(2,1)S(1)}, u32[]{:S(2)}, u32[]{:S(2)}) %all-to-all-start.1) | async-done | bytes 1048608 | tf_op jit(solution)/shard_map/all_to_all | solution.py:61
  105.0 0.7 copy.22
  105.7 1.4 %copy.21 = bf16[4,128,2,1,512]{4,0,2,1,3:T(4,128)(2,1)} copy(bf16[4,128,2,1,512]{4,2,0,1,3:T(2,128)(2,1)S(1)} %bitcast.39) | data formatting | bytes 2097152 | tf_op jit(solution)/shard_map/all_to_all | solution.py:61
  107.1 0.7 reshape_reshape.3
  107.8 0.4 reshape.80
  108.2 2.3 %slice_negate_fusion = (bf16[1024,1,2,1,128]{4,3,2,0,1:T(2,128)(2,1)S(1)}, bf16[1024,1,2,1,128]{4,3,2,0,1:T(2,128)(2,1)S(1)}) fusion(bf16[1024,1,2,2,128]{4,3,2,0,1:T(2,128)(2,1)S(1)} %reshape_reshape.3), kind=kLoop, calls=%fused_computation.6 | loop fusion | flops 262144 | bytes 2097152 | tf_op jit(solution)/shard_map/neg | solution.py:35
  110.6 2.4 %pad_maximum_fusion.1 = bf16[1024,1,2,2,128]{4,3,2,0,1:T(2,128)(2,1)S(1)} fusion(bf16[1024,1,2,1,128]{4,3,2,0,1:T(2,128)(2,1)S(1)} %get-tuple-element.8, bf16[1024,1,2,1,128]{4,3,2,0,1:T(2,128)(2,1)S(1)} %get-tuple-element.7), kind=kLoop, calls=%fused_computation.7 | loop fusion | flops 2097152 | bytes 2097152 | tf_op jit(solution)/shard_map/stack | solution.py:35
  113.0 0.4 reshape.81
  113.5 1.8 %constant_dynamic-slice_fusion = bf16[1,256,1,512]{3,0,1,2:T(2,128)(2,1)S(1)} fusion(bf16[4,256,1,512]{3,0,1,2:T(4,128)(2,1)} %bitcast.42, s32[]{:T(128)S(6)} %select_n.46), kind=kLoop, calls=%fused_computation.81 | loop fusion | bytes 524292 | tf_op jit(solution)/shard_map/jit(dynamic_index_in_dim)/dynamic_slice | solution.py:63
  115.2 0.1 pad_maximum_fusion
  115.4 2.1 %multiply_bitcast_fusion = f32[1,2,256,1024]{3,2,1,0:T(8,128)} fusion(bf16[2,1024,512]{2,1,0:T(8,128)(2,1)S(1)} %bitcast.40, bf16[1,256,1,512]{3,0,1,2:T(2,128)(2,1)S(1)} %constant_dynamic-slice_fusion), kind=kOutput, calls=%fused_computation.1 | convolution fusion | flops 537395200 | bytes 4456448 | tf_op jit(solution)/shard_map/cik,cjk->cij/dot_general | solution.py:41
  (5 shorter events, 0.1 us)
Async XLA Ops:
  27.8 77.2 %all-to-all-start.1 = ((bf16[4,2,128,512]{3,1,0,2:T(2,128)(2,1)}), bf16[4,2,128,512]{3,1,0,2:T(2,128)(2,1)S(1)}, u32[]{:S(2)}, u32[]{:S(2)}) async-start(bf16[4,2,128,512]{3,1,0,2:T(2,128)(2,1)} %copy.20), calls=%async_computation.1 | async-start | bytes 2097152 | tf_op jit(solution)/shard_map/all_to_all | solution.py:61
